TPU v7x, 512 devices: a whole 4x4x16 slice. The times are simulated.
512 devices in a mesh: rows: 128 (over z, y, core), grp: 4 (over x).
Axes of the slice: x: 4, y: 4, z: 16, core: 2. Of those that a mesh axis runs over, the one named last changes fastest.
Arguments:
- slab: bfloat16 [294912, 4096], P(('rows', 'grp')), may hold values from -24 to 24
- sketch: bfloat16 [4096, 128], replicated, may hold values from -0.09375 to 0.09375
Outputs:
- basis: float32 [294912, 128], P(('rows', 'grp'))
- projected: bfloat16 [4096, 128], P(('rows', 'grp'))
All inputs are finite; a program needn't handle non-finite values.
Results may differ from a plain program's by a relative error of at most 0.0035.
Values sent between devices are 32-bit elements; how exact they have to be, the bound alone decides.
A program may use at most 64 MiB of HBM per device.

v0:
```python
import jax
import jax.numpy as jnp
from jax import lax
from jax.sharding import PartitionSpec as P


def right_solve(matrix, gram):
    lower = jnp.linalg.cholesky(gram)
    return lax.linalg.triangular_solve(lower, matrix, left_side=False, lower=True, transpose_a=True)


def local_gram(matrix):
    return jnp.dot(
        matrix.T, matrix, precision=lax.Precision.HIGHEST, preferred_element_type=jnp.float32
    )


def orthonormal(matrix):
    gram = lax.psum(local_gram(matrix), ("rows", "grp"))
    result = right_solve(matrix, gram)
    return result


def local(slab, sketch):
    rows_loc, width = slab.shape
    devices_all = lax.axis_size(("rows", "grp"))
    total_rows = rows_loc * devices_all
    own_rows = width // devices_all
    first = jnp.dot(slab, sketch, preferred_element_type=jnp.float32)
    basis_one = orthonormal(first)
    low_one = basis_one.astype(jnp.bfloat16)
    whole = lax.psum(
        lax.dot_general(
            slab, low_one, (((0,), (0,)), ((), ())), preferred_element_type=jnp.float32
        ),
        ("rows", "grp"),
    )
    final = lax.dynamic_slice_in_dim(whole, lax.axis_index(("rows", "grp")) * own_rows, own_rows, 0)
    basis = basis_one * jnp.sqrt(jnp.float32(total_rows))
    projected = (final * jnp.sqrt(jnp.float32(width) / jnp.float32(total_rows))).astype(
        jnp.bfloat16
    )
    return (basis, projected)


def solution(mesh):
    return jax.shard_map(
        local,
        mesh=mesh,
        in_specs=(P(("rows", "grp"), None), P()),
        out_specs=(P(("rows", "grp"), None), P(("rows", "grp"), None)),
        check_vma=False,
    )
```

profile of v0, /device:TPU:1, one launch (start us, length us, event | category | flops | bytes accessed | tf_op | source)
XLA Modules:
  0.0 965.0 jit_solution(3742445075268766550)
XLA Ops:
  7.2 0.0 copy-start
  7.2 0.0 all-reduce.3.cloned.1.call-start
  7.2 1.2 copy-done
  8.4 3.7 fusion.5
  12.1 1.3 fusion.6
  13.4 0.0 all-reduce.3.cloned.1.call-update
  13.5 0.0 all-reduce.5.cloned.1.call-start
  13.5 445.5 %all-reduce.3.cloned.1.call-done = f32[128,128]{0,1:T(8,128)} async-done(((f32[128,128]{0,1:T(8,128)}), f32[128,128]{0,1:T(8,128)}) %all-reduce.3.cloned.1.call-update) | async-done | bytes 65552 | tf_op jit(solution)/shard_map/psum | solution.py:19
  459.0 0.9 copy.5
  460.0 0.9 fusion.4
  460.8 11.7 %cholesky.16 = f32[128,128]{1,0:T(8,128)S(1)} custom-call(f32[128,128]{1,0:T(8,128)S(1)} %fusion.4), custom_call_target="Cholesky" | custom-call | tf_op jit(solution)/shard_map/jit(cholesky)/cholesky | solution.py:8
  472.6 0.6 compare_reduce_fusion
  473.2 0.7 fusion.1
  473.9 9.8 %custom-call.6 = f32[1,128,128]{1,2,0:T(8,128)S(1)} custom-call(f32[1,128,128]{2,1,0:T(8,128)S(1)} %fusion.1), custom_call_target="InvertDiagBlocksLowerTriangular" | custom-call | tf_op jit(solution)/shard_map/triangular_solve | solution.py:9
  483.7 1.1 broadcast_multiply_fusion
  484.8 4.6 convolution_bitcast_fusion
  489.4 0.0 all-reduce.5.cloned.1.call-update
  489.5 467.1 %all-reduce.5.cloned.1.call-done = f32[4096,128]{0,1:T(8,128)} async-done(((f32[4096,128]{0,1:T(8,128)}), f32[4096,128]{0,1:T(8,128)}) %all-reduce.5.cloned.1.call-update) | async-done | bytes 2097168 | tf_op jit(solution)/shard_map/psum | solution.py:32
  956.6 0.9 multiply_convert_fusion
  957.5 0.7 copy.6
  (1 shorter events, 0.0 us)
Async XLA Ops:
  7.2 1.2 copy-start
  7.2 451.9 %all-reduce.3.cloned.1.call-start = ((), (), s32[]{:S(2)}) async-start(), calls=%async_computation | async-start | bytes 131072 | tf_op jit(solution)/shard_map/psum | solution.py:19
  13.5 943.1 %all-reduce.5.cloned.1.call-start = ((), (), s32[]{:S(2)}) async-start(), calls=%async_computation.1 | async-start | bytes 4194304 | tf_op jit(solution)/shard_map/psum | solution.py:32
Sparse Core Ops, SparseCore 0:
  14.0 444.9 all-reduce.2
  489.6 466.9 all-reduce.4
where the time goes:
time: 965 us
  waiting for transfers between devices  913 us (95%)
  other arithmetic  24.6 us (3%)
  between operations  14.1 us (1%)
  matrix products  10.8 us (1%)
    psum x1, waiting for transfers between devices, local(): lax.psum(lax.dot_general(slab, low_one, (((0,), (0,)), ((), ())), preferr...  467 us
    psum x1, waiting for transfers between devices, orthonormal(): gram = lax.psum(local_gram(matrix), ('rows', 'grp'))  446 us
  transfers between devices with their start and end apart: 2, of which 2 were waited for; matrix products, arithmetic and copies ran while one was open for 0% of the time, Pallas kernels for 0%

commit v1 on v0

v1 whole, which is shorter than its diff:
```python
import jax
import jax.numpy as jnp
from jax import lax
from jax.experimental import pallas as pl
from jax.experimental.pallas import tpu as pltpu
from jax.sharding import PartitionSpec as P

MESH = pl.DeviceIdType.MESH
F32, BF16 = jnp.float32, jnp.bfloat16
NZ, NY, NX = 16, 4, 4
LOADS = 4


def place(z, y, c, x):
    return {"rows": (z * NY + y) * 2 + c, "grp": x}


def wait_bytes(ref, sem):
    pltpu.make_async_copy(ref, ref, sem).wait()


def exchange(
    slab, sketch, first, gram, final,
    slab_v, sketch_v, first_t, part, got0, got1, sum1, got2, sum2, got3,
    gram0, gotg1, gotg2,
    load_sem, send_sem, recv0, recv1, recv2, recv3, recvg,
):
    rows_at, x = lax.axis_index("rows"), lax.axis_index("grp")
    z, y, c = rows_at // (2 * NY), (rows_at // 2) % NY, rows_at % 2
    rows = slab.shape[0]
    step = rows // LOADS

    barrier = pltpu.get_barrier_semaphore()
    peers = [
        (z, (y + dy) % NY, (c + dc) % 2, (x + dx) % NX)
        for dy in range(NY) for dx in range(NX) for dc in range(2) if (dy, dx, dc) != (0, 0, 0)
    ] + [((z + d) % NZ, y, c, x) for d in range(1, NZ)]
    for peer in peers:
        pl.semaphore_signal(barrier, inc=1, device_id=place(*peer), device_id_type=MESH)

    sketch_copy = pltpu.make_async_copy(sketch, sketch_v, load_sem.at[LOADS])
    sketch_copy.start()
    loads = [
        pltpu.make_async_copy(slab.at[pl.ds(i * step, step)], slab_v.at[pl.ds(i * step, step)], load_sem.at[i])
        for i in range(LOADS)
    ]
    for load in loads:
        load.start()
    sketch_copy.wait()
    for i, load in enumerate(loads):
        load.wait()
        first[pl.ds(i * step, step), :] = jnp.dot(
            slab_v[pl.ds(i * step, step), :], sketch_v[...], preferred_element_type=F32
        )

    whole = first[...]
    whole_t = whole.T
    local = jnp.dot(whole_t, whole, precision=lax.Precision.HIGHEST, preferred_element_type=F32)
    for q in range(16):
        gram0[q] = local[8 * q : 8 * q + 8, :]
    high = whole_t.astype(BF16)
    low = (whole_t - high.astype(F32)).astype(BF16)
    first_t[...] = jnp.concatenate([high, low], 0)

    pl.semaphore_wait(barrier, len(peers))

    def send(src, dst, at, recv, peer):
        copy = pltpu.make_async_remote_copy(
            src_ref=src, dst_ref=dst, send_sem=send_sem.at[at], recv_sem=recv,
            device_id=place(*peer), device_id_type=MESH,
        )
        copy.start()

    own = y * NX + x
    for dy in range(NY):
        for dx in range(NX):
            ty, tx = (y + dy) % NY, (x + dx) % NX
            slot = (dy * NX + dx) * 2
            if (dy, dx) != (0, 0):
                send(gram0.at[ty * NX + tx], gotg1.at[slot + c], 0, recvg.at[0], (z, ty, 0, tx))

    @pl.when(c == 1)
    def _():
        send(gram0.at[own], gotg1.at[1], 0, recvg.at[0], (z, y, 0, x))

    @pl.when(c == 0)
    def _():
        gotg1[0] = gram0[own]

    wide = 512
    for j in range(8):
        both = jnp.dot(first_t[...], slab_v[:, j * wide : (j + 1) * wide], preferred_element_type=F32)
        sums = both[:128] + both[128:]
        for k in range(4):
            block = sums[:, k * 128 : (k + 1) * 128].T
            at_z, half = (2 * j + k // 2), j // 4
            for yl in range(2):
                for cc in range(2):
                    for xx in range(4):
                        row = ((yl * 2 + cc) * 4 + xx) * 8
                        yy = 2 * (k % 2) + yl
                        a, b = (xx, yy) if half == 0 else (yy, xx)
                        part[cc, half, a, b, at_z % 8] = block[row : row + 8, :]
        if j % 4 == 3:
            half = j // 4
            send(part.at[1 - c, half], got0.at[half], 1 + half, recv0.at[half], (z, y, 1 - c, x))

    @pl.when(c == 0)
    def _():
        wait_bytes(gotg1.at[pl.ds(0, 31)], recvg.at[0])
        tile = gotg1[0]
        for s in range(1, 32):
            tile = tile + gotg1[s]
        gotg2[z] = tile
        for d in range(1, NZ):
            send(gotg2.at[z], gotg2.at[z], 3, recvg.at[1], ((z + d) % NZ, y, c, x))

    def peer_of(half, phase, d):
        if (half + phase) % 2 == 0:
            return (z, y, c, (x + d) % NX)
        return (z, (y + d) % NY, c, x)

    def index_of(half, phase, d):
        return (x + d) % NX if (half + phase) % 2 == 0 else (y + d) % NY

    for half in range(2):
        wait_bytes(got0.at[half], recv0.at[half])
        for d in (2, 1, 3, 0):
            a = index_of(half, 0, d)
            part[c, half, a] = part[c, half, a] + got0[half, a]
            if d:
                send(part.at[c, half, a], got1.at[half, d - 1], 4 + half, recv1.at[half], peer_of(half, 0, d))

    for half in range(2):
        wait_bytes(got1.at[half], recv1.at[half])
        a = index_of(half, 0, 0)
        for d in (2, 1, 3, 0):
            b = index_of(half, 1, d)
            sum1[half, b] = (part[c, half, a, b] + got1[half, 0, b]) + (got1[half, 1, b] + got1[half, 2, b])
            if d:
                send(sum1.at[half, b], got2.at[half, d - 1], 6 + half, recv2.at[half], peer_of(half, 1, d))

    for half in range(2):
        wait_bytes(got2.at[half], recv2.at[half])
        b = index_of(half, 1, 0)
        sum2[pl.ds(8 * half, 8)] = (sum1[half, b] + got2[half, 0]) + (got2[half, 1] + got2[half, 2])

    for d in range(1, NZ):
        to = (z + d) % NZ
        send(sum2.at[to], got3.at[d - 1], 8, recv3.at[0], (to, y, c, x))

    @pl.when(c == 0)
    def _():
        wait_bytes(gotg2.at[pl.ds(0, 15)], recvg.at[1])
        tile = gotg2[0]
        for s in range(1, NZ):
            tile = tile + gotg2[s]
        gram[own] = tile
        for dy in range(NY):
            for dx in range(NX):
                for cc in range(2):
                    if (dy, dx, cc) != (0, 0, 0):
                        send(gram.at[own], gram.at[own], 9, recvg.at[2], (z, (y + dy) % NY, cc, (x + dx) % NX))
        wait_bytes(gram.at[pl.ds(0, 15)], recvg.at[2])

    @pl.when(c == 1)
    def _():
        wait_bytes(gram, recvg.at[2])

    wait_bytes(got3, recv3.at[0])
    total = sum2[z]
    for d in range(NZ - 1):
        total = total + got3[d]
    final[...] = total

    @pl.when(c == 0)
    def _():
        wait_bytes(gram0.at[pl.ds(0, 15)], send_sem.at[0])
        wait_bytes(gotg2.at[pl.ds(0, 15)], send_sem.at[3])
        wait_bytes(gotg1.at[pl.ds(0, 31)], send_sem.at[9])

    @pl.when(c == 1)
    def _():
        wait_bytes(gram0, send_sem.at[0])

    for half in range(2):
        wait_bytes(got0.at[half], send_sem.at[1 + half])
        wait_bytes(got1.at[half], send_sem.at[4 + half])
        wait_bytes(got2.at[half], send_sem.at[6 + half])
    wait_bytes(got3, send_sem.at[8])


def local(slab, sketch):
    rows, width = slab.shape
    rank = sketch.shape[1]
    total_rows = rows * lax.axis_size(("rows", "grp"))
    vmem = pl.BlockSpec(memory_space=pltpu.VMEM)
    tiles = lambda *lead: pltpu.VMEM((*lead, 8, 128), F32)
    first, gram, final = pl.pallas_call(
        exchange,
        out_shape=[
            jax.ShapeDtypeStruct((rows, rank), F32),
            jax.ShapeDtypeStruct((16, 8, 128), F32),
            jax.ShapeDtypeStruct((8, 128), F32),
        ],
        in_specs=[pl.BlockSpec(memory_space=pl.ANY)] * 2,
        out_specs=[vmem] * 3,
        scratch_shapes=[
            pltpu.VMEM((rows, width), BF16),
            pltpu.VMEM((width, rank), BF16),
            pltpu.VMEM((2 * rank, rows), BF16),
            tiles(2, 2, 4, 4, 8),
            tiles(2, 4, 4, 8),
            tiles(2, 3, 4, 8),
            tiles(2, 4, 8),
            tiles(2, 3, 8),
            tiles(16),
            tiles(15),
            tiles(16),
            tiles(32),
            tiles(16),
            pltpu.SemaphoreType.DMA((LOADS + 1,)),
            pltpu.SemaphoreType.DMA((10,)),
            pltpu.SemaphoreType.DMA((2,)),
            pltpu.SemaphoreType.DMA((2,)),
            pltpu.SemaphoreType.DMA((2,)),
            pltpu.SemaphoreType.DMA((1,)),
            pltpu.SemaphoreType.DMA((3,)),
        ],
        compiler_params=pltpu.CompilerParams(
            collective_id=0, has_side_effects=True, vmem_limit_bytes=56 * 2**20
        ),
    )(slab, sketch)
    lower = jnp.linalg.cholesky(gram.reshape(rank, rank))
    solve = lambda m: lax.linalg.triangular_solve(lower, m, left_side=False, lower=True, transpose_a=True)
    both = solve(jnp.concatenate([first, final], 0))
    basis = both[:rows] * jnp.sqrt(jnp.float32(total_rows))
    projected = (both[rows:] * jnp.sqrt(jnp.float32(width) / jnp.float32(total_rows))).astype(BF16)
    return (basis, projected)


def solution(mesh):
    return jax.shard_map(
        local,
        mesh=mesh,
        in_specs=(P(("rows", "grp"), None), P()),
        out_specs=(P(("rows", "grp"), None), P(("rows", "grp"), None)),
        check_vma=False,
    )
```

time: 965 us -> 69.2 us (0.07)
  waiting for transfers between devices: 913 us -> 0 us
  Pallas kernels: 0 us -> 40.8 us
  between operations: 14.1 us -> 0.67 us
    psum x2 -> x0, waiting for transfers between devices: 913 us -> none  [the longest x1 467 us: local(): lax.psum(lax.dot_general(slab, low_one, (((0,), (0,)), ((), ())), preferr...]
    pallas_call x0 -> x1, Pallas kernels: none -> 40.8 us  [local(): pl.pallas_call(exchange, out_shape=[jax.ShapeDtypeStruct((rows, rank), F3...]
    dot_general x3 -> x0, matrix products: 9.7 us -> none  [the longest x1 4.65 us: local(): lax.dot_general(slab, low_one, (((0,), (0,)), ((), ())), preferred_elemen...]
  transfers between devices with their start and end apart: 2 -> 0, of which waited for: 2 -> 0; matrix products, arithmetic and copies ran while one was open for 0% -> 0% of each run, Pallas kernels for 0% -> 0%
where the time goes in v1:
time: 69.2 us; the launch traced here: 69 us
  Pallas kernels  40.8 us (59%)
  other arithmetic  25 us (36%)
  matrix products  1.58 us (2%)
  local copies, waits for them, and re-layouts  0.93 us (1%)
    pallas_call x1, Pallas kernels, local(): pl.pallas_call(exchange, out_shape=[jax.ShapeDtypeStruct((rows, rank), F3...  40.8 us
    another operation x3, other arithmetic, local(): lower = jnp.linalg.cholesky(gram.reshape(rank, rank))  12.4 us
    another operation x2, other arithmetic, local(): lax.linalg.triangular_solve(lower, m, left_side=False, lower=True, transp...  10.5 us
    another operation x1, matrix products, local(): lax.linalg.triangular_solve(lower, m, left_side=False, lower=True, transp...  1.58 us

profile of v1, /device:TPU:1, one launch (start us, length us, event | category | flops | bytes accessed | tf_op | source)
XLA Modules:
  0.0 69.0 jit_solution(15418123652414765196)
XLA Ops:
  0.6 40.8 %shard_map.41 = (f32[576,128]{1,0:T(8,128)}, f32[16,8,128]{2,1,0:T(8,128)}, f32[8,128]{1,0:T(8,128)}) custom-call(bf16[576,4096]{1,0:T(8,128)(2,1)} %slab.1, bf16[4096,128]{1,0:T(8,128)(2,1)} %sketch.1), custom_call_target="tpu_custom_call" | custom-call | tf_op jit(solution)/shard_map/pallas_call | solution.py:199
  41.4 0.9 %copy.6 = f32[128,128]{0,1:T(8,128)S(1)} copy(f32[128,128]{1,0:T(8,128)} %bitcast.11) | data formatting | bytes 131072 | tf_op jit(solution)/shard_map/reshape | solution.py:234
  42.3 0.9 %fusion.6 = f32[128,128]{1,0:T(8,128)S(1)} fusion(f32[128,128]{0,1:T(8,128)S(1)} %copy.6, f32[16,8,128]{2,1,0:T(8,128)} %get-tuple-element.7), kind=kLoop, calls=%fused_computation.9 | loop fusion | flops 32768 | bytes 196608 | tf_op jit(solution)/shard_map/jit(cholesky)/div | solution.py:234
  43.2 11.7 %cholesky.16 = f32[128,128]{1,0:T(8,128)S(1)} custom-call(f32[128,128]{1,0:T(8,128)S(1)} %fusion.6), custom_call_target="Cholesky" | custom-call | tf_op jit(solution)/shard_map/jit(cholesky)/cholesky | solution.py:234
  54.9 0.6 compare_reduce_fusion
  55.6 0.7 fusion.4
  56.2 9.8 %custom-call.6 = f32[1,128,128]{1,2,0:T(8,128)S(1)} custom-call(f32[1,128,128]{2,1,0:T(8,128)S(1)} %fusion.4), custom_call_target="InvertDiagBlocksLowerTriangular" | custom-call | tf_op jit(solution)/shard_map/triangular_solve | solution.py:235
  66.1 1.6 %fusion = f32[584,128]{1,0:T(8,128)S(1)} fusion(f32[8,128]{1,0:T(8,128)} %get-tuple-element.6, f32[576,128]{1,0:T(8,128)} %get-tuple-element.5, f32[1,128,128]{1,2,0:T(8,128)S(1)} %custom-call.6), kind=kOutput, calls=%fused_computation | convolution fusion | flops 114893824 | bytes 663552 | tf_op jit(solution)/shard_map/triangular_solve | solution.py:235
  67.6 0.6 fusion.7
  68.2 0.7 %slice_multiply_fusion = f32[576,128]{1,0:T(8,128)} fusion(f32[584,128]{1,0:T(8,128)S(1)} %fusion), kind=kLoop, calls=%fused_computation.4 | loop fusion | flops 73728 | bytes 589824 | tf_op jit(solution)/shard_map/mul | solution.py:237
  (1 shorter events, 0.0 us)

commit v2 on v1

--- a/solution.py
+++ b/solution.py
@@ -1,3 +1,6 @@
+import functools
+import math
+
 import jax
 import jax.numpy as jnp
 from jax import lax
@@ -19,10 +22,65 @@
     pltpu.make_async_copy(ref, ref, sem).wait()
 
 
+def lanes(tile, at):
+    return jnp.broadcast_to(tile[:, at : at + 1], tile.shape)
+
+
+def sublanes(tile, at):
+    return jnp.broadcast_to(tile[at : at + 1, :], tile.shape)
+
+
+def inverse_factor(gram):
+    blocks = len(gram)
+    shape = gram[0].shape
+    row = lax.broadcasted_iota(jnp.int32, shape, 0)
+    column = lax.broadcasted_iota(jnp.int32, shape, 1)
+    left = list(gram)
+    right = [jnp.where(column == row + 8 * i, 1.0, 0.0).astype(F32) for i in range(blocks)]
+    out = []
+    for b in range(blocks):
+        tile, unit = left[b], right[b]
+        cols = [lanes(tile, 8 * b + j) for j in range(8)]
+        pivots = jnp.zeros(shape, F32)
+        steps = []
+        for j in range(8):
+            pivot = sublanes(cols[j], j)
+            pivots = jnp.where(row == j, pivot, pivots)
+            inverse = 1.0 / pivot
+            rest = {l: sublanes(cols[l], j) for l in range(j + 1, 8)}
+            steps.append((inverse, sublanes(tile, j), sublanes(unit, j), rest))
+            if j < 7:
+                factor = jnp.where(row > j, cols[j] * inverse, 0.0)
+                tile = tile - factor * steps[j][1]
+                unit = unit - factor * steps[j][2]
+                for l in rest:
+                    cols[l] = cols[l] - factor * rest[l]
+        out.append(unit * lax.rsqrt(pivots))
+        for i in range(b + 1, blocks):
+            cols = [lanes(left[i], 8 * b + j) for j in range(8)]
+            for j, (inverse, tile_row, unit_row, rest) in enumerate(steps):
+                factor = cols[j] * inverse
+                left[i] = left[i] - factor * tile_row
+                right[i] = right[i] - factor * unit_row
+                for l in rest:
+                    cols[l] = cols[l] - factor * rest[l]
+    return out
+
+
+def finish(basis_scale, projected_scale, first, inverse, final, basis, projected):
+    def apply(matrix):
+        return lax.dot_general(
+            matrix, inverse[...], (((1,), (1,)), ((), ())), precision=lax.Precision.HIGHEST, preferred_element_type=F32
+        )
+
+    basis[...] = apply(first[...]) * basis_scale
+    projected[...] = (apply(final[...]) * projected_scale).astype(BF16)
+
+
 def exchange(
-    slab, sketch, first, gram, final,
+    slab, sketch, first, inverse, final,
     slab_v, sketch_v, first_t, part, got0, got1, sum1, got2, sum2, got3,
-    gram0, gotg1, gotg2,
+    gram0, gotg1, gotg2, gram,
     load_sem, send_sem, recv0, recv1, recv2, recv3, recvg,
 ):
     rows_at, x = lax.axis_index("rows"), lax.axis_index("grp")
@@ -167,6 +225,9 @@
     def _():
         wait_bytes(gram, recvg.at[2])
 
+    for i, tile in enumerate(inverse_factor([gram[q] for q in range(16)])):
+        inverse[8 * i : 8 * i + 8, :] = tile
+
     wait_bytes(got3, recv3.at[0])
     total = sum2[z]
     for d in range(NZ - 1):
@@ -196,11 +257,11 @@
     total_rows = rows * lax.axis_size(("rows", "grp"))
     vmem = pl.BlockSpec(memory_space=pltpu.VMEM)
     tiles = lambda *lead: pltpu.VMEM((*lead, 8, 128), F32)
-    first, gram, final = pl.pallas_call(
+    first, inverse, final = pl.pallas_call(
         exchange,
         out_shape=[
             jax.ShapeDtypeStruct((rows, rank), F32),
-            jax.ShapeDtypeStruct((16, 8, 128), F32),
+            jax.ShapeDtypeStruct((rank, rank), F32),
             jax.ShapeDtypeStruct((8, 128), F32),
         ],
         in_specs=[pl.BlockSpec(memory_space=pl.ANY)] * 2,
@@ -219,6 +280,7 @@
             tiles(16),
             tiles(32),
             tiles(16),
+            tiles(16),
             pltpu.SemaphoreType.DMA((LOADS + 1,)),
             pltpu.SemaphoreType.DMA((10,)),
             pltpu.SemaphoreType.DMA((2,)),
@@ -231,11 +293,10 @@
             collective_id=0, has_side_effects=True, vmem_limit_bytes=56 * 2**20
         ),
     )(slab, sketch)
-    lower = jnp.linalg.cholesky(gram.reshape(rank, rank))
-    solve = lambda m: lax.linalg.triangular_solve(lower, m, left_side=False, lower=True, transpose_a=True)
-    both = solve(jnp.concatenate([first, final], 0))
-    basis = both[:rows] * jnp.sqrt(jnp.float32(total_rows))
-    projected = (both[rows:] * jnp.sqrt(jnp.float32(width) / jnp.float32(total_rows))).astype(BF16)
+    basis, projected = pl.pallas_call(
+        functools.partial(finish, math.sqrt(total_rows), math.sqrt(width / total_rows)),
+        out_shape=[jax.ShapeDtypeStruct((rows, rank), F32), jax.ShapeDtypeStruct((8, 128), BF16)],
+    )(first, inverse, final)
     return (basis, projected)
 
 

time: 69.2 us -> 47.6 us (0.69)
  other arithmetic: 25 us -> 0 us
  Pallas kernels: 40.8 us -> 46.9 us
  matrix products: 1.58 us -> 0 us
  local copies, waits for them, and re-layouts: 0.93 us -> 0 us
    another operation x5 -> x0, other arithmetic: 22.9 us -> none  [the longest x3 12.4 us: local(): lower = jnp.linalg.cholesky(gram.reshape(rank, rank))]
    pallas_call x1, Pallas kernels: 40.8 us -> 44.6 us  [local(): pl.pallas_call(exchange, out_shape=[jax.ShapeDtypeStruct((rows, rank), F3...]
    pallas_call x0 -> x1, Pallas kernels: none -> 2.22 us  [local(): pl.pallas_call(functools.partial(finish, math.sqrt(total_rows), math.sqrt...]
    another operation x1 -> x0, matrix products: 1.58 us -> none  [local(): lax.linalg.triangular_solve(lower, m, left_side=False, lower=True, transp...]
    reshape x1 -> x0, local copies, waits for them, and re-layouts: 0.93 us -> none  [local(): lower = jnp.linalg.cholesky(gram.reshape(rank, rank))]
    div x1 -> x0, other arithmetic: 0.85 us -> none  [local(): lower = jnp.linalg.cholesky(gram.reshape(rank, rank))]
    mul x1 -> x0, other arithmetic: 0.74 us -> none  [local(): basis = both[:rows] * jnp.sqrt(jnp.float32(total_rows))]
where the time goes in v2:
time: 47.6 us; the launch traced here: 47.5 us
  Pallas kernels  46.9 us (99%)
  between operations  0.64 us (1%)
    pallas_call x1, Pallas kernels, local(): pl.pallas_call(exchange, out_shape=[jax.ShapeDtypeStruct((rows, rank), F3...  44.6 us
    pallas_call x1, Pallas kernels, local(): pl.pallas_call(functools.partial(finish, math.sqrt(total_rows), math.sqrt...  2.22 us

profile of v2, /device:TPU:1, one launch (start us, length us, event | category | flops | bytes accessed | tf_op | source)
XLA Modules:
  0.0 47.5 jit_solution(15534108420738919826)
XLA Ops:
  0.6 44.6 %shard_map.41 = (f32[576,128]{1,0:T(8,128)}, f32[128,128]{1,0:T(8,128)}, f32[8,128]{1,0:T(8,128)}) custom-call(bf16[576,4096]{1,0:T(8,128)(2,1)} %slab.1, bf16[4096,128]{1,0:T(8,128)(2,1)} %sketch.1), custom_call_target="tpu_custom_call" | custom-call | tf_op jit(solution)/shard_map/pallas_call | solution.py:260
  45.3 2.2 %shard_map.42 = (f32[576,128]{1,0:T(8,128)}, bf16[8,128]{1,0:T(8,128)(2,1)}) custom-call(f32[576,128]{1,0:T(8,128)} %get-tuple-element.5.first, f32[128,128]{1,0:T(8,128)} %get-tuple-element.6.inverse, f32[8,128]{1,0:T(8,128)} %get-tuple-element.7.final), custom_call_target="tpu_custom_call" | custom-call | tf_op jit(solution)/shard_map/pallas_call | solution.py:296

commit v3 on v2

--- a/solution.py
+++ b/solution.py
@@ -78,23 +78,26 @@
 
 
 def exchange(
-    slab, sketch, first, inverse, final,
-    slab_v, sketch_v, first_t, part, got0, got1, sum1, got2, sum2, got3,
+    slab, sketch, first_out, inverse, final,
+    slab_v, sketch_v, first, first_t, part, got0, got1, sum1, got2, sum2, got3,
     gram0, gotg1, gotg2, gram,
-    load_sem, send_sem, recv0, recv1, recv2, recv3, recvg,
+    load_sem, send_sem, recv0, recv1, recv2, recv3, recvg, ready,
 ):
     rows_at, x = lax.axis_index("rows"), lax.axis_index("grp")
     z, y, c = rows_at // (2 * NY), (rows_at // 2) % NY, rows_at % 2
     rows = slab.shape[0]
     step = rows // LOADS
 
-    barrier = pltpu.get_barrier_semaphore()
-    peers = [
-        (z, (y + dy) % NY, (c + dc) % 2, (x + dx) % NX)
-        for dy in range(NY) for dx in range(NX) for dc in range(2) if (dy, dx, dc) != (0, 0, 0)
-    ] + [((z + d) % NZ, y, c, x) for d in range(1, NZ)]
-    for peer in peers:
-        pl.semaphore_signal(barrier, inc=1, device_id=place(*peer), device_id_type=MESH)
+    def send(src, dst, at, recv, peer):
+        pltpu.make_async_remote_copy(
+            src_ref=src, dst_ref=dst, send_sem=send_sem.at[at], recv_sem=recv,
+            device_id=place(*peer), device_id_type=MESH,
+        ).start()
+
+    def hops(dy, dx):
+        return min(dy, NY - dy) + min(dx, NX - dx)
+
+    chips = sorted(((dy, dx) for dy in range(NY) for dx in range(NX)), key=lambda d: -hops(*d))
 
     sketch_copy = pltpu.make_async_copy(sketch, sketch_v, load_sem.at[LOADS])
     sketch_copy.start()
@@ -104,12 +107,23 @@
     ]
     for load in loads:
         load.start()
+
+    barrier = pltpu.get_barrier_semaphore()
+    peers = [((z + d) % NZ, y, c, x) for d in (4, 12, 3, 13, 2, 14, 1, 15)] + [
+        (z, (y + dy) % NY, (c + dc) % 2, (x + dx) % NX)
+        for dy, dx in chips for dc in range(2) if (dy, dx, dc) != (0, 0, 0)
+    ]
+    for peer in peers:
+        pl.semaphore_signal(barrier, inc=1, device_id=place(*peer), device_id_type=MESH)
+
     sketch_copy.wait()
     for i, load in enumerate(loads):
         load.wait()
         first[pl.ds(i * step, step), :] = jnp.dot(
             slab_v[pl.ds(i * step, step), :], sketch_v[...], preferred_element_type=F32
         )
+    store = pltpu.make_async_copy(first, first_out, load_sem.at[LOADS + 1])
+    store.start()
 
     whole = first[...]
     whole_t = whole.T
@@ -120,22 +134,36 @@
     low = (whole_t - high.astype(F32)).astype(BF16)
     first_t[...] = jnp.concatenate([high, low], 0)
 
+    def product(half):
+        wide = 512
+        for j in range(4 * half, 4 * half + 4):
+            both = jnp.dot(first_t[...], slab_v[:, j * wide : (j + 1) * wide], preferred_element_type=F32)
+            sums = both[:128] + both[128:]
+            for k in range(4):
+                block = sums[:, k * 128 : (k + 1) * 128].T
+                at_z = 2 * j + k // 2
+                for yl in range(2):
+                    for cc in range(2):
+                        for xx in range(4):
+                            row = ((yl * 2 + cc) * 4 + xx) * 8
+                            yy = 2 * (k % 2) + yl
+                            a, b = (xx, yy) if half == 0 else (yy, xx)
+                            part[cc, half, a, b, at_z % 8] = block[row : row + 8, :]
+
+    def to_core(half):
+        send(part.at[1 - c, half], got0.at[half], 1 + half, recv0.at[half], (z, y, 1 - c, x))
+
+    product(0)
+
     pl.semaphore_wait(barrier, len(peers))
-
-    def send(src, dst, at, recv, peer):
-        copy = pltpu.make_async_remote_copy(
-            src_ref=src, dst_ref=dst, send_sem=send_sem.at[at], recv_sem=recv,
-            device_id=place(*peer), device_id_type=MESH,
-        )
-        copy.start()
+    for d in (4, 12):
+        pl.semaphore_signal(ready, inc=1, device_id=place((z + d) % NZ, y, c, x), device_id_type=MESH)
 
     own = y * NX + x
-    for dy in range(NY):
-        for dx in range(NX):
-            ty, tx = (y + dy) % NY, (x + dx) % NX
-            slot = (dy * NX + dx) * 2
-            if (dy, dx) != (0, 0):
-                send(gram0.at[ty * NX + tx], gotg1.at[slot + c], 0, recvg.at[0], (z, ty, 0, tx))
+    for dy, dx in chips:
+        ty, tx = (y + dy) % NY, (x + dx) % NX
+        if (dy, dx) != (0, 0):
+            send(gram0.at[ty * NX + tx], gotg1.at[(dy * NX + dx) * 2 + c], 0, recvg.at[0], (z, ty, 0, tx))
 
     @pl.when(c == 1)
     def _():
@@ -145,33 +173,9 @@
     def _():
         gotg1[0] = gram0[own]
 
-    wide = 512
-    for j in range(8):
-        both = jnp.dot(first_t[...], slab_v[:, j * wide : (j + 1) * wide], preferred_element_type=F32)
-        sums = both[:128] + both[128:]
-        for k in range(4):
-            block = sums[:, k * 128 : (k + 1) * 128].T
-            at_z, half = (2 * j + k // 2), j // 4
-            for yl in range(2):
-                for cc in range(2):
-                    for xx in range(4):
-                        row = ((yl * 2 + cc) * 4 + xx) * 8
-                        yy = 2 * (k % 2) + yl
-                        a, b = (xx, yy) if half == 0 else (yy, xx)
-                        part[cc, half, a, b, at_z % 8] = block[row : row + 8, :]
-        if j % 4 == 3:
-            half = j // 4
-            send(part.at[1 - c, half], got0.at[half], 1 + half, recv0.at[half], (z, y, 1 - c, x))
-
-    @pl.when(c == 0)
-    def _():
-        wait_bytes(gotg1.at[pl.ds(0, 31)], recvg.at[0])
-        tile = gotg1[0]
-        for s in range(1, 32):
-            tile = tile + gotg1[s]
-        gotg2[z] = tile
-        for d in range(1, NZ):
-            send(gotg2.at[z], gotg2.at[z], 3, recvg.at[1], ((z + d) % NZ, y, c, x))
+    to_core(0)
+    product(1)
+    to_core(1)
 
     def peer_of(half, phase, d):
         if (half + phase) % 2 == 0:
@@ -188,6 +192,20 @@
             part[c, half, a] = part[c, half, a] + got0[half, a]
             if d:
                 send(part.at[c, half, a], got1.at[half, d - 1], 4 + half, recv1.at[half], peer_of(half, 0, d))
+
+    pl.semaphore_wait(ready, 2)
+
+    @pl.when(c == 0)
+    def _():
+        wait_bytes(gotg1.at[pl.ds(0, 31)], recvg.at[0])
+        tile = gotg1[0]
+        for s in range(1, 32):
+            tile = tile + gotg1[s]
+        gotg2[z] = tile
+        for to in range(NZ):
+            @pl.when(z != to)
+            def _():
+                send(gotg2.at[z], gotg2.at[z], 3, recvg.at[1], (to, y, c, x))
 
     for half in range(2):
         wait_bytes(got1.at[half], recv1.at[half])
@@ -198,15 +216,6 @@
             if d:
                 send(sum1.at[half, b], got2.at[half, d - 1], 6 + half, recv2.at[half], peer_of(half, 1, d))
 
-    for half in range(2):
-        wait_bytes(got2.at[half], recv2.at[half])
-        b = index_of(half, 1, 0)
-        sum2[pl.ds(8 * half, 8)] = (sum1[half, b] + got2[half, 0]) + (got2[half, 1] + got2[half, 2])
-
-    for d in range(1, NZ):
-        to = (z + d) % NZ
-        send(sum2.at[to], got3.at[d - 1], 8, recv3.at[0], (to, y, c, x))
-
     @pl.when(c == 0)
     def _():
         wait_bytes(gotg2.at[pl.ds(0, 15)], recvg.at[1])
@@ -214,11 +223,22 @@
         for s in range(1, NZ):
             tile = tile + gotg2[s]
         gram[own] = tile
-        for dy in range(NY):
-            for dx in range(NX):
-                for cc in range(2):
-                    if (dy, dx, cc) != (0, 0, 0):
-                        send(gram.at[own], gram.at[own], 9, recvg.at[2], (z, (y + dy) % NY, cc, (x + dx) % NX))
+        for dy, dx in chips:
+            for cc in range(2):
+                if (dy, dx, cc) != (0, 0, 0):
+                    send(gram.at[own], gram.at[own], 9, recvg.at[2], (z, (y + dy) % NY, cc, (x + dx) % NX))
+
+    for half in range(2):
+        wait_bytes(got2.at[half], recv2.at[half])
+        b = index_of(half, 1, 0)
+        sum2[pl.ds(8 * half, 8)] = (sum1[half, b] + got2[half, 0]) + (got2[half, 1] + got2[half, 2])
+        for to in range(8 * half, 8 * half + 8):
+            @pl.when(z != to)
+            def _():
+                send(sum2.at[to], got3.at[z], 8, recv3.at[0], (to, y, c, x))
+
+    @pl.when(c == 0)
+    def _():
         wait_bytes(gram.at[pl.ds(0, 15)], recvg.at[2])
 
     @pl.when(c == 1)
@@ -228,10 +248,11 @@
     for i, tile in enumerate(inverse_factor([gram[q] for q in range(16)])):
         inverse[8 * i : 8 * i + 8, :] = tile
 
-    wait_bytes(got3, recv3.at[0])
-    total = sum2[z]
-    for d in range(NZ - 1):
-        total = total + got3[d]
+    got3[z] = sum2[z]
+    wait_bytes(got3.at[pl.ds(0, 15)], recv3.at[0])
+    total = got3[0]
+    for s in range(1, NZ):
+        total = total + got3[s]
     final[...] = total
 
     @pl.when(c == 0)
@@ -248,7 +269,8 @@
         wait_bytes(got0.at[half], send_sem.at[1 + half])
         wait_bytes(got1.at[half], send_sem.at[4 + half])
         wait_bytes(got2.at[half], send_sem.at[6 + half])
-    wait_bytes(got3, send_sem.at[8])
+    wait_bytes(got3.at[pl.ds(0, 15)], send_sem.at[8])
+    store.wait()
 
 
 def local(slab, sketch):
@@ -265,10 +287,11 @@
             jax.ShapeDtypeStruct((8, 128), F32),
         ],
         in_specs=[pl.BlockSpec(memory_space=pl.ANY)] * 2,
-        out_specs=[vmem] * 3,
+        out_specs=[pl.BlockSpec(memory_space=pl.ANY), vmem, vmem],
         scratch_shapes=[
             pltpu.VMEM((rows, width), BF16),
             pltpu.VMEM((width, rank), BF16),
+            pltpu.VMEM((rows, rank), F32),
             pltpu.VMEM((2 * rank, rows), BF16),
             tiles(2, 2, 4, 4, 8),
             tiles(2, 4, 4, 8),
@@ -276,18 +299,19 @@
             tiles(2, 4, 8),
             tiles(2, 3, 8),
             tiles(16),
-            tiles(15),
+            tiles(16),
             tiles(16),
             tiles(32),
             tiles(16),
             tiles(16),
-            pltpu.SemaphoreType.DMA((LOADS + 1,)),
+            pltpu.SemaphoreType.DMA((LOADS + 2,)),
             pltpu.SemaphoreType.DMA((10,)),
             pltpu.SemaphoreType.DMA((2,)),
             pltpu.SemaphoreType.DMA((2,)),
             pltpu.SemaphoreType.DMA((2,)),
             pltpu.SemaphoreType.DMA((1,)),
             pltpu.SemaphoreType.DMA((3,)),
+            pltpu.SemaphoreType.REGULAR,
         ],
         compiler_params=pltpu.CompilerParams(
             collective_id=0, has_side_effects=True, vmem_limit_bytes=56 * 2**20

time: 47.6 us -> 41.2 us (0.87)
  Pallas kernels: 46.9 us -> 40.4 us
    pallas_call x1, Pallas kernels: 44.6 us -> 38.2 us  [local(): pl.pallas_call(exchange, out_shape=[jax.ShapeDtypeStruct((rows, rank), F3...]
where the time goes in v3:
time: 41.2 us; the launch traced here: 41 us
  Pallas kernels  40.4 us (98%)
  between operations  0.64 us (2%)
    pallas_call x1, Pallas kernels, local(): pl.pallas_call(exchange, out_shape=[jax.ShapeDtypeStruct((rows, rank), F3...  38.2 us
    pallas_call x1, Pallas kernels, local(): pl.pallas_call(functools.partial(finish, math.sqrt(total_rows), math.sqrt...  2.22 us

profile of v3, /device:TPU:1, one launch (start us, length us, event | category | flops | bytes accessed | tf_op | source)
XLA Modules:
  0.0 41.0 jit_solution(17193182140215282958)
XLA Ops:
  0.6 38.2 %shard_map.41 = (f32[576,128]{1,0:T(8,128)}, f32[128,128]{1,0:T(8,128)}, f32[8,128]{1,0:T(8,128)}) custom-call(bf16[576,4096]{1,0:T(8,128)(2,1)} %slab.1, bf16[4096,128]{1,0:T(8,128)(2,1)} %sketch.1), custom_call_target="tpu_custom_call" | custom-call | tf_op jit(solution)/shard_map/pallas_call | solution.py:282
  38.8 2.2 %shard_map.42 = (f32[576,128]{1,0:T(8,128)}, bf16[8,128]{1,0:T(8,128)(2,1)}) custom-call(f32[576,128]{1,0:T(8,128)} %get-tuple-element.5.first, f32[128,128]{1,0:T(8,128)} %get-tuple-element.6.inverse, f32[8,128]{1,0:T(8,128)} %get-tuple-element.7.final), custom_call_target="tpu_custom_call" | custom-call | tf_op jit(solution)/shard_map/pallas_call | solution.py:320

commit v4 on v3

--- a/solution.py
+++ b/solution.py
@@ -78,8 +78,8 @@
 
 
 def exchange(
-    slab, sketch, first_out, inverse, final,
-    slab_v, sketch_v, first, first_t, part, got0, got1, sum1, got2, sum2, got3,
+    slab, sketch, first, inverse, final,
+    slab_v, sketch_v, first_t, part, got0, got1, sum1, got2, sum2, got3,
     gram0, gotg1, gotg2, gram,
     load_sem, send_sem, recv0, recv1, recv2, recv3, recvg, ready,
 ):
@@ -122,8 +122,6 @@
         first[pl.ds(i * step, step), :] = jnp.dot(
             slab_v[pl.ds(i * step, step), :], sketch_v[...], preferred_element_type=F32
         )
-    store = pltpu.make_async_copy(first, first_out, load_sem.at[LOADS + 1])
-    store.start()
 
     whole = first[...]
     whole_t = whole.T
@@ -134,26 +132,56 @@
     low = (whole_t - high.astype(F32)).astype(BF16)
     first_t[...] = jnp.concatenate([high, low], 0)
 
-    def product(half):
-        wide = 512
-        for j in range(4 * half, 4 * half + 4):
-            both = jnp.dot(first_t[...], slab_v[:, j * wide : (j + 1) * wide], preferred_element_type=F32)
-            sums = both[:128] + both[128:]
-            for k in range(4):
-                block = sums[:, k * 128 : (k + 1) * 128].T
-                at_z = 2 * j + k // 2
-                for yl in range(2):
-                    for cc in range(2):
-                        for xx in range(4):
-                            row = ((yl * 2 + cc) * 4 + xx) * 8
-                            yy = 2 * (k % 2) + yl
-                            a, b = (xx, yy) if half == 0 else (yy, xx)
-                            part[cc, half, a, b, at_z % 8] = block[row : row + 8, :]
-
-    def to_core(half):
-        send(part.at[1 - c, half], got0.at[half], 1 + half, recv0.at[half], (z, y, 1 - c, x))
-
-    product(0)
+    def product(j):
+        both = jnp.dot(first_t[...], slab_v[:, j * 512 : (j + 1) * 512], preferred_element_type=F32)
+        sums = both[:128] + both[128:]
+        for k in range(4):
+            block = sums[:, k * 128 : (k + 1) * 128].T
+            for yl in range(2):
+                for cc in range(2):
+                    for xx in range(4):
+                        row = ((yl * 2 + cc) * 4 + xx) * 8
+                        yy = 2 * (k % 2) + yl
+                        a, b = (xx, yy) if j % 2 == 0 else (yy, xx)
+                        part[cc, j, a, b, k // 2] = block[row : row + 8, :]
+
+    def peer_of(j, phase, d):
+        if (j + phase) % 2 == 0:
+            return (z, y, c, (x + d) % NX)
+        return (z, (y + d) % NY, c, x)
+
+    def index_of(j, phase, d):
+        return (x + d) % NX if (j + phase) % 2 == 0 else (y + d) % NY
+
+    def to_core(j):
+        send(part.at[1 - c, j], got0.at[j], 1, recv0.at[j], (z, y, 1 - c, x))
+
+    def to_first_axis(j):
+        wait_bytes(got0.at[j], recv0.at[j])
+        for d in (2, 1, 3, 0):
+            a = index_of(j, 0, d)
+            part[c, j, a] = part[c, j, a] + got0[j, a]
+            if d:
+                send(part.at[c, j, a], got1.at[j, d - 1], 2, recv1.at[j], peer_of(j, 0, d))
+
+    def to_second_axis(j):
+        wait_bytes(got1.at[j], recv1.at[j])
+        a = index_of(j, 0, 0)
+        for d in (2, 1, 3, 0):
+            b = index_of(j, 1, d)
+            sum1[j, b] = (part[c, j, a, b] + got1[j, 0, b]) + (got1[j, 1, b] + got1[j, 2, b])
+            if d:
+                send(sum1.at[j, b], got2.at[j, d - 1], 4, recv2.at[j], peer_of(j, 1, d))
+
+    def to_planes(j):
+        wait_bytes(got2.at[j], recv2.at[j])
+        b = index_of(j, 1, 0)
+        sum2[pl.ds(2 * j, 2)] = (sum1[j, b] + got2[j, 0]) + (got2[j, 1] + got2[j, 2])
+        for to in range(2 * j, 2 * j + 2):
+            @pl.when(z != to)
+            def _():
+                send(sum2.at[to], got3.at[z], 5, recv3.at[0], (to, y, c, x))
+
 
     pl.semaphore_wait(barrier, len(peers))
     for d in (4, 12):
@@ -173,25 +201,14 @@
     def _():
         gotg1[0] = gram0[own]
 
-    to_core(0)
-    product(1)
-    to_core(1)
-
-    def peer_of(half, phase, d):
-        if (half + phase) % 2 == 0:
-            return (z, y, c, (x + d) % NX)
-        return (z, (y + d) % NY, c, x)
-
-    def index_of(half, phase, d):
-        return (x + d) % NX if (half + phase) % 2 == 0 else (y + d) % NY
-
-    for half in range(2):
-        wait_bytes(got0.at[half], recv0.at[half])
-        for d in (2, 1, 3, 0):
-            a = index_of(half, 0, d)
-            part[c, half, a] = part[c, half, a] + got0[half, a]
-            if d:
-                send(part.at[c, half, a], got1.at[half, d - 1], 4 + half, recv1.at[half], peer_of(half, 0, d))
+    for j in range(8):
+        product(j)
+        to_core(j)
+        if j >= 4:
+            to_first_axis(j - 4)
+
+    for j in range(4, 4):
+        to_first_axis(j)
 
     pl.semaphore_wait(ready, 2)
 
@@ -207,14 +224,13 @@
             def _():
                 send(gotg2.at[z], gotg2.at[z], 3, recvg.at[1], (to, y, c, x))
 
-    for half in range(2):
-        wait_bytes(got1.at[half], recv1.at[half])
-        a = index_of(half, 0, 0)
-        for d in (2, 1, 3, 0):
-            b = index_of(half, 1, d)
-            sum1[half, b] = (part[c, half, a, b] + got1[half, 0, b]) + (got1[half, 1, b] + got1[half, 2, b])
-            if d:
-                send(sum1.at[half, b], got2.at[half, d - 1], 6 + half, recv2.at[half], peer_of(half, 1, d))
+    for j in range(4, 8):
+        to_first_axis(j)
+
+    for j in range(8):
+        to_second_axis(j)
+    for j in range(4):
+        to_planes(j)
 
     @pl.when(c == 0)
     def _():
@@ -226,16 +242,10 @@
         for dy, dx in chips:
             for cc in range(2):
                 if (dy, dx, cc) != (0, 0, 0):
-                    send(gram.at[own], gram.at[own], 9, recvg.at[2], (z, (y + dy) % NY, cc, (x + dx) % NX))
-
-    for half in range(2):
-        wait_bytes(got2.at[half], recv2.at[half])
-        b = index_of(half, 1, 0)
-        sum2[pl.ds(8 * half, 8)] = (sum1[half, b] + got2[half, 0]) + (got2[half, 1] + got2[half, 2])
-        for to in range(8 * half, 8 * half + 8):
-            @pl.when(z != to)
-            def _():
-                send(sum2.at[to], got3.at[z], 8, recv3.at[0], (to, y, c, x))
+                    send(gram.at[own], gram.at[own], 6, recvg.at[2], (z, (y + dy) % NY, cc, (x + dx) % NX))
+
+    for j in range(4, 8):
+        to_planes(j)
 
     @pl.when(c == 0)
     def _():
@@ -259,18 +269,16 @@
     def _():
         wait_bytes(gram0.at[pl.ds(0, 15)], send_sem.at[0])
         wait_bytes(gotg2.at[pl.ds(0, 15)], send_sem.at[3])
-        wait_bytes(gotg1.at[pl.ds(0, 31)], send_sem.at[9])
+        wait_bytes(gotg1.at[pl.ds(0, 31)], send_sem.at[6])
 
     @pl.when(c == 1)
     def _():
         wait_bytes(gram0, send_sem.at[0])
 
-    for half in range(2):
-        wait_bytes(got0.at[half], send_sem.at[1 + half])
-        wait_bytes(got1.at[half], send_sem.at[4 + half])
-        wait_bytes(got2.at[half], send_sem.at[6 + half])
-    wait_bytes(got3.at[pl.ds(0, 15)], send_sem.at[8])
-    store.wait()
+    wait_bytes(got0, send_sem.at[1])
+    wait_bytes(got1, send_sem.at[2])
+    wait_bytes(got2, send_sem.at[4])
+    wait_bytes(got3.at[pl.ds(0, 15)], send_sem.at[5])
 
 
 def local(slab, sketch):
@@ -281,46 +289,42 @@
     tiles = lambda *lead: pltpu.VMEM((*lead, 8, 128), F32)
     first, inverse, final = pl.pallas_call(
         exchange,
-        out_shape=[
-            jax.ShapeDtypeStruct((rows, rank), F32),
-            jax.ShapeDtypeStruct((rank, rank), F32),
-            jax.ShapeDtypeStruct((8, 128), F32),
-        ],
+        out_shape=[pltpu.VMEM((rows, rank), F32), pltpu.VMEM((rank, rank), F32), pltpu.VMEM((8, 128), F32)],
         in_specs=[pl.BlockSpec(memory_space=pl.ANY)] * 2,
-        out_specs=[pl.BlockSpec(memory_space=pl.ANY), vmem, vmem],
+        out_specs=[vmem] * 3,
         scratch_shapes=[
             pltpu.VMEM((rows, width), BF16),
             pltpu.VMEM((width, rank), BF16),
-            pltpu.VMEM((rows, rank), F32),
             pltpu.VMEM((2 * rank, rows), BF16),
-            tiles(2, 2, 4, 4, 8),
-            tiles(2, 4, 4, 8),
-            tiles(2, 3, 4, 8),
-            tiles(2, 4, 8),
-            tiles(2, 3, 8),
+            tiles(2, 8, 4, 4, 2),
+            tiles(8, 4, 4, 2),
+            tiles(8, 3, 4, 2),
+            tiles(8, 4, 2),
+            tiles(8, 3, 2),
             tiles(16),
             tiles(16),
             tiles(16),
             tiles(32),
             tiles(16),
             tiles(16),
-            pltpu.SemaphoreType.DMA((LOADS + 2,)),
-            pltpu.SemaphoreType.DMA((10,)),
-            pltpu.SemaphoreType.DMA((2,)),
-            pltpu.SemaphoreType.DMA((2,)),
-            pltpu.SemaphoreType.DMA((2,)),
+            pltpu.SemaphoreType.DMA((LOADS + 1,)),
+            pltpu.SemaphoreType.DMA((7,)),
+            pltpu.SemaphoreType.DMA((8,)),
+            pltpu.SemaphoreType.DMA((8,)),
+            pltpu.SemaphoreType.DMA((8,)),
             pltpu.SemaphoreType.DMA((1,)),
             pltpu.SemaphoreType.DMA((3,)),
             pltpu.SemaphoreType.REGULAR,
         ],
         compiler_params=pltpu.CompilerParams(
-            collective_id=0, has_side_effects=True, vmem_limit_bytes=56 * 2**20
+            collective_id=0, has_side_effects=True, vmem_limit_bytes=24 * 2**20
         ),
-    )(slab, sketch)
+    )(*(pltpu.with_memory_space_constraint(array, pltpu.HBM) for array in (slab, sketch)))
     basis, projected = pl.pallas_call(
         functools.partial(finish, math.sqrt(total_rows), math.sqrt(width / total_rows)),
         out_shape=[jax.ShapeDtypeStruct((rows, rank), F32), jax.ShapeDtypeStruct((8, 128), BF16)],
-    )(first, inverse, final)
+        compiler_params=pltpu.CompilerParams(vmem_limit_bytes=8 * 2**20),
+    )(*(pltpu.with_memory_space_constraint(array, pltpu.VMEM) for array in (first, inverse, final)))
     return (basis, projected)
 
 

time: 41.2 us -> 38.6 us (0.937)
  Pallas kernels: 40.4 us -> 37.8 us
    pallas_call x1, Pallas kernels: 38.2 us -> 36.6 us  [local(): pl.pallas_call(exchange, out_shape=[pltpu.VMEM((rows, rank), F32), pltpu....]
    pallas_call x1, Pallas kernels: 2.22 us -> 1.22 us  [local(): pl.pallas_call(functools.partial(finish, math.sqrt(total_rows), math.sqrt...]
where the time goes in v4:
time: 38.6 us; the launch traced here: 38.5 us
  Pallas kernels  37.8 us (98%)
  between operations  0.64 us (2%)
    pallas_call x1, Pallas kernels, local(): pl.pallas_call(exchange, out_shape=[pltpu.VMEM((rows, rank), F32), pltpu....  36.6 us
    pallas_call x1, Pallas kernels, local(): pl.pallas_call(functools.partial(finish, math.sqrt(total_rows), math.sqrt...  1.22 us

profile of v4, /device:TPU:1, one launch (start us, length us, event | category | flops | bytes accessed | tf_op | source)
XLA Modules:
  0.0 38.5 jit_solution(14733684733861183992)
XLA Ops:
  0.6 36.6 %shard_map.41 = (f32[576,128]{1,0:T(8,128)S(1)}, f32[128,128]{1,0:T(8,128)S(1)}, f32[8,128]{1,0:T(8,128)S(1)}) custom-call(bf16[576,4096]{1,0:T(8,128)(2,1)} %slab.1, bf16[4096,128]{1,0:T(8,128)(2,1)} %sketch.1), custom_call_target="tpu_custom_call" | custom-call | tf_op jit(solution)/shard_map/pallas_call | solution.py:290
  37.2 1.2 %shard_map.42 = (f32[576,128]{1,0:T(8,128)}, bf16[8,128]{1,0:T(8,128)(2,1)}) custom-call(f32[576,128]{1,0:T(8,128)S(1)} %get-tuple-element.5.first, f32[128,128]{1,0:T(8,128)S(1)} %get-tuple-element.6.inverse, f32[8,128]{1,0:T(8,128)S(1)} %get-tuple-element.7.final), custom_call_target="tpu_custom_call" | custom-call | tf_op jit(solution)/shard_map/pallas_call | solution.py:323

commit v5 on v4

--- a/solution.py
+++ b/solution.py
@@ -77,6 +77,11 @@
     projected[...] = (apply(final[...]) * projected_scale).astype(BF16)
 
 
+def owner_of(tile):
+    at = tile // 2 + 1
+    return (at // 3 + 3) % NY, tile % 2, (at % 3 + 3) % NX
+
+
 def exchange(
     slab, sketch, first, inverse, final,
     slab_v, sketch_v, first_t, part, got0, got1, sum1, got2, sum2, got3,
@@ -187,19 +192,24 @@
     for d in (4, 12):
         pl.semaphore_signal(ready, inc=1, device_id=place((z + d) % NZ, y, c, x), device_id_type=MESH)
 
-    own = y * NX + x
-    for dy, dx in chips:
-        ty, tx = (y + dy) % NY, (x + dx) % NX
-        if (dy, dx) != (0, 0):
-            send(gram0.at[ty * NX + tx], gotg1.at[(dy * NX + dx) * 2 + c], 0, recvg.at[0], (z, ty, 0, tx))
-
-    @pl.when(c == 1)
-    def _():
-        send(gram0.at[own], gotg1.at[1], 0, recvg.at[0], (z, y, 0, x))
-
-    @pl.when(c == 0)
-    def _():
-        gotg1[0] = gram0[own]
+    at_y, at_x = (y + 1) % NY, (x + 1) % NX
+    is_owner = (at_y < 3) & (at_x < 3) & (at_y + at_x > 0)
+    own = 2 * (3 * at_y + at_x - 1) + c
+    slot = (y * NX + x) * 2 + c
+
+    def unless_here(to_y, to_c, to_x):
+        return pl.when((y != to_y) | (x != to_x) | (c != to_c))
+
+    for q in (14, 15, 12, 13, 8, 9, 2, 3, 10, 11, 6, 7, 4, 5, 0, 1):
+        to = owner_of(q)
+
+        @unless_here(*to)
+        def _():
+            send(gram0.at[q], gotg1.at[slot], 0, recvg.at[0], (z, *to))
+
+    @pl.when(is_owner)
+    def _():
+        gotg1[slot] = gram0[own]
 
     for j in range(8):
         product(j)
@@ -212,7 +222,7 @@
 
     pl.semaphore_wait(ready, 2)
 
-    @pl.when(c == 0)
+    @pl.when(is_owner)
     def _():
         wait_bytes(gotg1.at[pl.ds(0, 31)], recvg.at[0])
         tile = gotg1[0]
@@ -232,26 +242,27 @@
     for j in range(4):
         to_planes(j)
 
-    @pl.when(c == 0)
+    @pl.when(is_owner)
     def _():
         wait_bytes(gotg2.at[pl.ds(0, 15)], recvg.at[1])
         tile = gotg2[0]
         for s in range(1, NZ):
             tile = tile + gotg2[s]
         gram[own] = tile
-        for dy, dx in chips:
-            for cc in range(2):
-                if (dy, dx, cc) != (0, 0, 0):
-                    send(gram.at[own], gram.at[own], 6, recvg.at[2], (z, (y + dy) % NY, cc, (x + dx) % NX))
+        for to_y, to_x in sorted(((v, u) for v in range(NY) for u in range(NX)), key=sum):
+            for to_c in (1, 0):
+                @unless_here(to_y, to_c, to_x)
+                def _():
+                    send(gram.at[own], gram.at[own], 6, recvg.at[2], (z, to_y, to_c, to_x))
 
     for j in range(4, 8):
         to_planes(j)
 
-    @pl.when(c == 0)
+    @pl.when(is_owner)
     def _():
         wait_bytes(gram.at[pl.ds(0, 15)], recvg.at[2])
 
-    @pl.when(c == 1)
+    @pl.when(jnp.logical_not(is_owner))
     def _():
         wait_bytes(gram, recvg.at[2])
 
@@ -265,13 +276,13 @@
         total = total + got3[s]
     final[...] = total
 
-    @pl.when(c == 0)
+    @pl.when(is_owner)
     def _():
         wait_bytes(gram0.at[pl.ds(0, 15)], send_sem.at[0])
         wait_bytes(gotg2.at[pl.ds(0, 15)], send_sem.at[3])
         wait_bytes(gotg1.at[pl.ds(0, 31)], send_sem.at[6])
 
-    @pl.when(c == 1)
+    @pl.when(jnp.logical_not(is_owner))
     def _():
         wait_bytes(gram0, send_sem.at[0])
 

time: 38.6 us -> 37.7 us (0.977)
  Pallas kernels: 37.8 us -> 36.9 us
    pallas_call x1, Pallas kernels: 36.6 us -> 35.7 us  [local(): pl.pallas_call(exchange, out_shape=[pltpu.VMEM((rows, rank), F32), pltpu....]
where the time goes in v5:
time: 37.7 us; the launch traced here: 37.6 us
  Pallas kernels  36.9 us (98%)
  between operations  0.64 us (2%)
    pallas_call x1, Pallas kernels, local(): pl.pallas_call(exchange, out_shape=[pltpu.VMEM((rows, rank), F32), pltpu....  35.7 us
    pallas_call x1, Pallas kernels, local(): pl.pallas_call(functools.partial(finish, math.sqrt(total_rows), math.sqrt...  1.22 us

profile of v5, /device:TPU:1, one launch (start us, length us, event | category | flops | bytes accessed | tf_op | source)
XLA Modules:
  0.0 37.6 jit_solution(10678181178178502037)
XLA Ops:
  0.6 35.7 %shard_map.41 = (f32[576,128]{1,0:T(8,128)S(1)}, f32[128,128]{1,0:T(8,128)S(1)}, f32[8,128]{1,0:T(8,128)S(1)}) custom-call(bf16[576,4096]{1,0:T(8,128)(2,1)} %slab.1, bf16[4096,128]{1,0:T(8,128)(2,1)} %sketch.1), custom_call_target="tpu_custom_call" | custom-call | tf_op jit(solution)/shard_map/pallas_call | solution.py:301
  36.3 1.2 %shard_map.42 = (f32[576,128]{1,0:T(8,128)}, bf16[8,128]{1,0:T(8,128)(2,1)}) custom-call(f32[576,128]{1,0:T(8,128)S(1)} %get-tuple-element.5.first, f32[128,128]{1,0:T(8,128)S(1)} %get-tuple-element.6.inverse, f32[8,128]{1,0:T(8,128)S(1)} %get-tuple-element.7.final), custom_call_target="tpu_custom_call" | custom-call | tf_op jit(solution)/shard_map/pallas_call | solution.py:334

commit v6 on v5

--- a/solution.py
+++ b/solution.py
@@ -36,41 +36,57 @@
     row = lax.broadcasted_iota(jnp.int32, shape, 0)
     column = lax.broadcasted_iota(jnp.int32, shape, 1)
     left = list(gram)
-    right = [jnp.where(column == row + 8 * i, 1.0, 0.0).astype(F32) for i in range(blocks)]
     out = []
     for b in range(blocks):
-        tile, unit = left[b], right[b]
+        tile = left[b]
         cols = [lanes(tile, 8 * b + j) for j in range(8)]
-        pivots = jnp.zeros(shape, F32)
-        steps = []
+        here = (column >= 8 * b) & (column < 8 * b + 8)
+        tile = jnp.where(here, jnp.where(column == row + 8 * b, 1.0, 0.0), tile)
+        own = {(i, l): sublanes(cols[l], i) for i in range(8) for l in range(i, 8)}
+        over, factor = {}, {}
         for j in range(8):
-            pivot = sublanes(cols[j], j)
-            pivots = jnp.where(row == j, pivot, pivots)
-            inverse = 1.0 / pivot
-            rest = {l: sublanes(cols[l], j) for l in range(j + 1, 8)}
-            steps.append((inverse, sublanes(tile, j), sublanes(unit, j), rest))
-            if j < 7:
-                factor = jnp.where(row > j, cols[j] * inverse, 0.0)
-                tile = tile - factor * steps[j][1]
-                unit = unit - factor * steps[j][2]
-                for l in rest:
-                    cols[l] = cols[l] - factor * rest[l]
-        out.append(unit * lax.rsqrt(pivots))
+            over[j] = 1.0 / own[j, j]
+            for i in range(j + 1, 8):
+                factor[i, j] = own[j, i] * over[j]
+            for i in range(j + 1, 8):
+                for l in range(i, 8):
+                    own[i, l] = own[i, l] - factor[i, j] * own[j, l]
+        rows = [sublanes(tile, j) for j in range(8)]
+        for j in range(8):
+            for i in range(j + 1, 8):
+                rows[i] = rows[i] - factor[i, j] * rows[j]
+        pivots, done = own[0, 0], rows[0]
+        for j in range(1, 8):
+            pivots = jnp.where(row == j, own[j, j], pivots)
+            done = jnp.where(row == j, rows[j], done)
+        out.append(jnp.where(column < 8 * b + 8, done * lax.rsqrt(pivots), 0.0))
         for i in range(b + 1, blocks):
             cols = [lanes(left[i], 8 * b + j) for j in range(8)]
-            for j, (inverse, tile_row, unit_row, rest) in enumerate(steps):
-                factor = cols[j] * inverse
-                left[i] = left[i] - factor * tile_row
-                right[i] = right[i] - factor * unit_row
-                for l in rest:
-                    cols[l] = cols[l] - factor * rest[l]
+            rest = jnp.where(here, 0.0, left[i])
+            for j in range(8):
+                times = cols[j] * over[j]
+                for l in range(j + 1, 8):
+                    cols[l] = cols[l] - times * own[j, l]
+                rest = rest - times * rows[j]
+            left[i] = rest
     return out
 
 
+def thirds(matrix):
+    high = matrix.astype(BF16)
+    rest = matrix - high.astype(F32)
+    middle = rest.astype(BF16)
+    return high, middle, (rest - middle.astype(F32)).astype(BF16)
+
+
 def finish(basis_scale, projected_scale, first, inverse, final, basis, projected):
+    high, middle, low = thirds(inverse[...])
+    right = jnp.concatenate([high, high, middle, high, middle, low], 1)
+
     def apply(matrix):
+        h, m, l = thirds(matrix)
         return lax.dot_general(
-            matrix, inverse[...], (((1,), (1,)), ((), ())), precision=lax.Precision.HIGHEST, preferred_element_type=F32
+            jnp.concatenate([h, m, h, l, m, h], 1), right, (((1,), (1,)), ((), ())), preferred_element_type=F32
         )
 
     basis[...] = apply(first[...]) * basis_scale

time: 37.7 us -> 37.6 us (level)
  no operation moved by 1% of the time
where the time goes in v6:
time: 37.6 us; the launch traced here: 37.5 us
  Pallas kernels  36.8 us (98%)
  between operations  0.64 us (2%)
    pallas_call x1, Pallas kernels, local(): pl.pallas_call(exchange, out_shape=[pltpu.VMEM((rows, rank), F32), pltpu....  35.7 us
    pallas_call x1, Pallas kernels, local(): pl.pallas_call(functools.partial(finish, math.sqrt(total_rows), math.sqrt...  1.16 us

profile of v6, /device:TPU:1, one launch (start us, length us, event | category | flops | bytes accessed | tf_op | source)
XLA Modules:
  0.0 37.5 jit_solution(121141295299141591)
XLA Ops:
  0.6 35.7 %shard_map.41 = (f32[576,128]{1,0:T(8,128)S(1)}, f32[128,128]{1,0:T(8,128)S(1)}, f32[8,128]{1,0:T(8,128)S(1)}) custom-call(bf16[576,4096]{1,0:T(8,128)(2,1)} %slab.1, bf16[4096,128]{1,0:T(8,128)(2,1)} %sketch.1), custom_call_target="tpu_custom_call" | custom-call | tf_op jit(solution)/shard_map/pallas_call | solution.py:317
  36.3 1.2 %shard_map.42 = (f32[576,128]{1,0:T(8,128)}, bf16[8,128]{1,0:T(8,128)(2,1)}) custom-call(f32[576,128]{1,0:T(8,128)S(1)} %get-tuple-element.5.first, f32[128,128]{1,0:T(8,128)S(1)} %get-tuple-element.6.inverse, f32[8,128]{1,0:T(8,128)S(1)} %get-tuple-element.7.final), custom_call_target="tpu_custom_call" | custom-call | tf_op jit(solution)/shard_map/pallas_call | solution.py:350
